TPU v7x, 128 devices: a whole 4x4x4 slice. The times are simulated.
128 devices in a mesh: rep: 16 (over z, x_hi, core), sec: 2 (over x_lo), mdl: 4 (over y).
Axes of the slice: x: 4 (x_hi: 2, x_lo: 2; x = x_hi * 2 + x_lo), y: 4, z: 4, core: 2. Of those that a mesh axis runs over, the one named last changes fastest.
Arguments:
- obs: bfloat16 [2, 8192, 1536], P('sec', 'rep'), may hold values from -6 to 6
- a_query: bfloat16 [1536, 1536], P(None, 'mdl'), may hold values from -0.15309311 to 0.15309311
- a_keyval: bfloat16 [2, 1536, 512], P(None, None, 'mdl'), may hold values from -0.15309311 to 0.15309311
- a_out: bfloat16 [1536, 1536], P('mdl'), may hold values from -0.15625 to 0.15625
- w_policy: bfloat16 [1536, 128], replicated, may hold values from -0.15625 to 0.15625
- c_in: bfloat16 [1536, 2048], P(None, 'mdl'), may hold values from -0.15309311 to 0.15309311
- c_query: bfloat16 [2048, 2048], P(None, 'mdl'), may hold values from -0.13258252 to 0.13258252
- c_keyval: bfloat16 [2, 2048, 512], P(None, None, 'mdl'), may hold values from -0.13258252 to 0.13258252
- c_out: bfloat16 [2048, 2048], P('mdl'), may hold values from -0.125 to 0.125
- w_value: bfloat16 [2048], replicated, may hold values from -0.110485435 to 0.110485435
- actions: int32 [2, 8192], P('sec', 'rep'), may hold values from 0 to 127
- advantages: float32 [2, 8192], P('sec', 'rep'), may hold values from -6 to 6
- old_logp: float32 [2, 8192], P('sec', 'rep'), may hold values from -7 to -4
- returns: float32 [2, 8192], P('sec', 'rep'), may hold values from -6 to 6
- robot_count: int32 [2], replicated, may hold values from 2048 to 8192, as said below
Outputs:
- values: float32 [2, 8192], P('sec', ('rep', 'mdl'))
- grad_a_out: float32 [1536, 1536], P('mdl')
- grad_c_out: float32 [2048, 2048], P('mdl')
Inputs may be any that keep to these rules, and one draw needn't show every extreme that they name: `robot_count`: one of the two micro-batches holds all 8192 robots, the other at least 2048; live robots are the first ones.
All inputs are finite; a program needn't handle non-finite values.
Results may differ from a plain program's by a relative error of at most 0.023.
Values may be sent and summed in bfloat16 or wider, within the bound.
A program may use at most 128 MiB of HBM per device.

v0:
```python
import math
import jax
import jax.numpy as jnp
from jax import lax
from jax.sharding import PartitionSpec as P

HEAD = 128
epsilon = 1e-05
clip_range = 0.2
masked_score = -1e30


def rms_normed(values_in):
    return values_in * lax.rsqrt(jnp.mean(values_in * values_in, axis=-1, keepdims=True) + epsilon)


def norm_backward(source, normed, grad_in):
    factor = lax.rsqrt(jnp.mean(source * source, axis=-1, keepdims=True) + epsilon)
    return factor * (grad_in - normed * jnp.mean(grad_in * normed, axis=-1, keepdims=True))


def project(source, w_query, w_keyval):
    normed = rms_normed(source).astype(jnp.bfloat16)
    queries = (
        jnp.dot(normed, w_query, preferred_element_type=jnp.float32) * HEAD ** (-0.5)
    ).astype(jnp.bfloat16)
    keyval = jnp.einsum("rd,cdk->crk", normed, w_keyval, preferred_element_type=jnp.float32).astype(
        jnp.bfloat16
    )
    return (queries, keyval)


def policy_backward(hidden, action_ids, advantage, old_values, live_mask, live_total, w_policy):
    source = hidden.astype(jnp.float32)
    normed = rms_normed(source)
    logits = jnp.dot(normed.astype(jnp.bfloat16), w_policy, preferred_element_type=jnp.float32)
    log_probs = jax.nn.log_softmax(logits, axis=-1)
    onehot = (action_ids[:, None] == lax.broadcasted_iota(jnp.int32, logits.shape, 1)).astype(
        jnp.float32
    )
    chosen = jnp.sum(onehot * log_probs, axis=-1)
    prob_ratio = jnp.exp(chosen - old_values)
    plain_term = prob_ratio * advantage
    bounded = jnp.clip(prob_ratio, 1.0 - clip_range, 1.0 + clip_range) * advantage
    slope_term = jnp.where(
        live_mask & (plain_term <= bounded), -plain_term / live_total, jnp.float32(0.0)
    )
    dlogits = slope_term[:, None] * (onehot - jnp.exp(log_probs))
    dnormed = jnp.dot(dlogits, w_policy.astype(jnp.float32).T, precision=lax.Precision.HIGHEST)
    return norm_backward(source, normed, dnormed)


def value_backward(mixed_out, target, live_mask, live_total, w_value):
    normed = rms_normed(mixed_out)
    value_pred = jnp.dot(normed.astype(jnp.bfloat16), w_value, preferred_element_type=jnp.float32)
    slope_term = jnp.where(live_mask, value_pred - target, jnp.float32(0.0)) / live_total
    dnormed = slope_term[:, None] * w_value.astype(jnp.float32)[None, :]
    return (value_pred, norm_backward(mixed_out, normed, dnormed))


def split_heads(queries, kv_heads):
    row_count = queries.shape[0]
    groups = queries.shape[1] // HEAD // kv_heads
    return queries.reshape(row_count, kv_heads, groups, HEAD)


def start_state(heads_in):
    row_count, kv_heads, groups, _ = heads_in.shape
    row_top = jnp.full((kv_heads, groups, row_count), masked_score, jnp.float32)
    row_sum = jnp.zeros((kv_heads, groups, row_count), jnp.float32)
    acc_sum = jnp.zeros((kv_heads, groups, row_count, HEAD), jnp.float32)
    return (row_top, row_sum, acc_sum)


def make_fold(heads_in, robot_total, carried, piece):
    kv_heads = heads_in.shape[1]
    piece_rows = piece.shape[1]
    block_rows = math.gcd(piece_rows, 512)
    block_count = piece_rows // block_rows
    key_blocks = piece[0].reshape(block_count, block_rows, kv_heads, HEAD)
    value_blocks = piece[1].reshape(block_count, block_rows, kv_heads, HEAD)

    def absorb(inner, block_item):
        block_index, key_block, value_block = block_item
        first_key = block_index * block_rows
        row_top, row_sum, acc_sum = inner
        scores = jnp.einsum(
            "rkgd,jkd->kgrj", heads_in, key_block, preferred_element_type=jnp.float32
        )
        key_live = first_key + lax.iota(jnp.int32, block_rows) < robot_total
        scores = jnp.where(key_live, scores, masked_score)
        new_top = jnp.maximum(row_top, jnp.max(scores, axis=-1))
        rescale = jnp.exp(row_top - new_top)
        weights = jnp.exp(scores - new_top[..., None])
        row_sum = row_sum * rescale + jnp.sum(weights, axis=-1)
        value_float = value_block.astype(jnp.float32)
        acc_sum = acc_sum * rescale[..., None] + jnp.einsum(
            "kgrj,jkd->kgrd", weights, value_float, precision=lax.Precision.HIGHEST
        )
        return ((new_top, row_sum, acc_sum), None)

    result, _ = lax.scan(
        absorb, carried, (jnp.arange(block_count, dtype=jnp.int32), key_blocks, value_blocks)
    )
    return result


def finish_heads(carried):
    _, row_sum, acc_sum = carried
    combined = acc_sum / row_sum[..., None]
    kv_heads, groups, row_count, _ = combined.shape
    return (
        jnp.transpose(combined, (2, 0, 1, 3))
        .reshape(row_count, kv_heads * groups * HEAD)
        .astype(jnp.bfloat16)
    )


def on_device(
    obs,
    a_query,
    a_keyval,
    a_out,
    w_policy,
    c_in,
    c_query,
    c_keyval,
    c_out,
    w_value,
    actions,
    advantages,
    old_logp,
    returns,
    robot_count,
):
    row_count = obs.shape[1]
    batch_index = lax.axis_index("sec")
    robot_total = robot_count[batch_index]
    live_total = jnp.sum(robot_count).astype(jnp.float32)
    first_row = lax.axis_index("rep") * row_count
    live_mask = first_row + lax.iota(jnp.int32, row_count) < robot_total
    mdl_count = lax.axis_size("mdl")
    part_rows = row_count // mdl_count
    row_start = lax.axis_index("mdl") * part_rows
    obs_float = obs[0].astype(jnp.float32)
    queries, keyval = project(obs_float, a_query, a_keyval)
    heads_a = split_heads(queries, keyval.shape[2] // HEAD)
    state_a = make_fold(
        heads_a,
        robot_total,
        start_state(heads_a),
        lax.all_gather(keyval, "rep", axis=1, tiled=True),
    )
    attended = finish_heads(state_a)
    mixed_sum = lax.psum(jnp.dot(attended, a_out, preferred_element_type=jnp.float32), "mdl")
    hidden = (obs_float + mixed_sum).astype(jnp.bfloat16)
    dhidden = policy_backward(
        hidden, actions[0], advantages[0], old_logp[0], live_mask, live_total, w_policy
    ).astype(jnp.bfloat16)
    actor_grad = jnp.einsum("rh,rd->hd", attended, dhidden, preferred_element_type=jnp.float32)
    embed_part = jnp.dot(hidden, c_in, preferred_element_type=jnp.float32).astype(jnp.bfloat16)
    embedded = lax.all_gather(embed_part, "mdl", axis=1, tiled=True)
    embed_float = embedded.astype(jnp.float32)
    critic_queries, critic_keyval = project(embed_float, c_query, c_keyval)
    heads_c = split_heads(critic_queries, critic_keyval.shape[2] // HEAD)
    state_c = make_fold(
        heads_c,
        robot_total,
        start_state(heads_c),
        lax.all_gather(critic_keyval, "rep", axis=1, tiled=True),
    )
    critic_attended = finish_heads(state_c)
    critic_sum = lax.psum(
        jnp.dot(critic_attended, c_out, preferred_element_type=jnp.float32).astype(jnp.bfloat16),
        "mdl",
    ).astype(jnp.float32)
    value_pred, dmixed = value_backward(
        embed_float + critic_sum, returns[0], live_mask, live_total, w_value
    )
    value_part = lax.dynamic_slice_in_dim(value_pred, row_start, part_rows, 0)
    dmixed_all = dmixed.astype(jnp.bfloat16)
    critic_grad = jnp.einsum(
        "rh,rd->hd", critic_attended, dmixed_all, preferred_element_type=jnp.float32
    )
    actor_summed, critic_summed = (
        lax.psum(actor_grad.astype(jnp.bfloat16), ("rep", "sec")).astype(jnp.float32),
        lax.psum(critic_grad.astype(jnp.bfloat16), ("rep", "sec")).astype(jnp.float32),
    )
    return (value_part[None, :], actor_summed, critic_summed)


def solution(mesh):
    return jax.shard_map(
        on_device,
        mesh=mesh,
        in_specs=(
            P("sec", "rep", None),
            P(None, "mdl"),
            P(None, None, "mdl"),
            P("mdl", None),
            P(),
            P(None, "mdl"),
            P(None, "mdl"),
            P(None, None, "mdl"),
            P("mdl", None),
            P(),
            P("sec", "rep"),
            P("sec", "rep"),
            P("sec", "rep"),
            P("sec", "rep"),
            P(),
        ),
        out_specs=(P("sec", ("rep", "mdl")), P("mdl", None), P("mdl", None)),
        check_vma=False,
    )
```

profile of v0, /device:TPU:1, one launch (start us, length us, event | category | flops | bytes accessed | tf_op | source)
XLA Modules:
  0.0 878.9 jit_solution(12537995733930431458)
XLA Ops:
  17.4 53.9 %all-gather.4.cloned.1.call-done = bf16[2,8192,128]{2,1,0:T(8,128)(2,1)} async-done(((bf16[2,512,128]{2,1,0:T(8,128)(2,1)}), bf16[2,8192,128]{2,1,0:T(8,128)(2,1)}) %all-gather.4.cloned.1.call-update) | async-done | bytes 4194320 | tf_op jit(solution)/shard_map/all_gather | solution.py:152
  71.4 4.5 fusion.116
  75.9 188.8 %while.30 = (s32[]{:T(128)}, f32[1,3,512]{2,1,0:T(4,128)S(1)}, f32[1,3,512]{2,1,0:T(4,128)S(1)}, f32[1,3,512,128]{3,2,1,0:T(8,128)S(1)}, s32[16]{0:T(128)S(1)}, ...) while((s32[]{:T(128)}, f32[1,3,512]{2,1,0:T(4,128)S(1)}, ...), condition=%wide.region_4.5_spmd.clone, body=%wide.region_1.4_spmd.clone.sunk | while | flops 1415391232 | bytes 24348876 | solution.py:102
  95.5 3.9 fusion.148
  107.3 3.9 fusion.148
  119.1 3.9 fusion.148
  130.9 3.9 fusion.148
  267.0 3.9 fusion.118
  271.0 73.2 %all-reduce.5.cloned.1.call-done = f32[512,1536]{1,0:T(8,128)} async-done(((f32[512,1536]{1,0:T(8,128)}), f32[512,1536]{1,0:T(8,128)}) %all-reduce.5.cloned.1.call-update) | async-done | bytes 3145744 | tf_op jit(solution)/shard_map/psum | solution.py:155
  350.9 30.8 %all-gather.6.cloned.1.call-done = bf16[512,2048]{1,0:T(8,128)(2,1)} async-done(((bf16[512,512]{1,0:T(8,128)(2,1)}), bf16[512,2048]{1,0:T(8,128)(2,1)}) %all-gather.6.cloned.1.call-update) | async-done | bytes 2097168 | tf_op jit(solution)/shard_map/all_gather | solution.py:162
  387.1 4.4 fusion.84
  393.5 49.4 %all-gather.8.cloned.1.call-done = bf16[2,8192,128]{2,1,0:T(8,128)(2,1)} async-done(((bf16[2,512,128]{2,1,0:T(8,128)(2,1)}), bf16[2,8192,128]{2,1,0:T(8,128)(2,1)}) %all-gather.8.cloned.1.call-update) | async-done | bytes 4194320 | tf_op jit(solution)/shard_map/all_gather | solution.py:170
  442.8 4.5 fusion.115
  447.4 234.7 %while.31 = (s32[]{:T(128)}, f32[1,4,512]{2,1,0:T(4,128)S(1)}, f32[1,4,512]{2,1,0:T(4,128)}, f32[1,4,512,128]{3,2,1,0:T(8,128)S(1)}, s32[16]{0:T(128)S(1)}, /*in...) while((s32[]{:T(128)}, f32[1,4,512]{2,1,0:T(4,128)S(1)}, ...), condition=%wide.region_10.11_spmd.clone, body=%wide.region_7.10_spmd.clone.sunk | while | flops 1887187968 | bytes 32447348 | solution.py:102
  457.1 4.9 fusion.153
  471.7 4.9 fusion.153
  486.4 4.9 fusion.153
  501.1 4.9 fusion.153
  515.7 4.9 fusion.153
  530.4 4.9 fusion.153
  545.1 4.9 fusion.153
  559.7 4.9 fusion.153
  574.4 4.9 fusion.153
  589.1 4.9 fusion.153
  603.8 4.9 fusion.153
  618.4 4.9 fusion.153
  633.1 4.9 fusion.153
  647.8 4.9 fusion.153
  662.4 4.9 fusion.153
  677.1 4.9 fusion.153
  691.4 52.2 %all-reduce.7.cloned.1.call-done = bf16[512,2048]{1,0:T(8,128)(2,1)} async-done(((bf16[512,2048]{1,0:T(8,128)(2,1)}), bf16[512,2048]{1,0:T(8,128)(2,1)}) %all-reduce.7.cloned.1.call-update) | async-done | bytes 2097168 | tf_op jit(solution)/shard_map/psum | solution.py:173
  757.4 109.0 %all-reduce.9.cloned.1.call-done = (bf16[384,1536]{1,0:T(8,128)(2,1)}, bf16[512,2048]{1,0:T(8,128)(2,1)}) async-done(((bf16[384,1536]{1,0:T(8,128)(2,1)}, bf16[512,2048]{1,0:T(8,128)(2,1)}), (bf16[384,1536]{1,0:T(8,128)(2,1)}, bf16[512,2048]{1,0:T(8,128)(2,1)})) %all-reduce.9.cloned.1.call-update) | async-done | bytes 3276816 | tf_op jit(solution)/shard_map/psum | solution.py:186
  (584 shorter events, 359.9 us)
Async XLA Ops:
  7.2 677.6 %copy-start = (bf16[512,2048]{1,0:T(8,128)(2,1)S(1)}, bf16[512,2048]{1,0:T(8,128)(2,1)}, u32[]{:S(2)}) copy-start(bf16[512,2048]{1,0:T(8,128)(2,1)} %param.27) | copy-start | bytes 6291460
  7.2 64.2 %all-gather.4.cloned.1.call-start = ((), (), s32[]{:S(2)}) async-start(), calls=%async_computation | async-start | bytes 4456448 | tf_op jit(solution)/shard_map/all_gather | solution.py:152
  12.1 332.1 %all-reduce.5.cloned.1.call-start = ((), (), s32[]{:S(2)}) async-start(), calls=%async_computation.1 | async-start | bytes 6291456 | tf_op jit(solution)/shard_map/psum | solution.py:155
  271.0 110.7 %all-gather.6.cloned.1.call-start = ((), (), s32[]{:S(2)}) async-start(), calls=%async_computation.2 | async-start | bytes 2621440 | tf_op jit(solution)/shard_map/all_gather | solution.py:162
  349.0 34.7 %copy-start.20 = (bf16[2,2048,128]{2,1,0:T(8,128)(2,1)S(1)}, bf16[2,2048,128]{2,1,0:T(8,128)(2,1)}, u32[]{:S(2)}) copy-start(bf16[2,2048,128]{2,1,0:T(8,128)(2,1)} %param.26) | copy-start | bytes 3145732
  350.8 92.0 %all-gather.8.cloned.1.call-start = ((), (), s32[]{:S(2)}) async-start(), calls=%async_computation.3 | async-start | bytes 4456448 | tf_op jit(solution)/shard_map/all_gather | solution.py:170
  386.8 356.8 %all-reduce.7.cloned.1.call-start = ((), (), s32[]{:S(2)}) async-start(), calls=%async_computation.4 | async-start | bytes 4194304 | tf_op jit(solution)/shard_map/psum | solution.py:173
  456.8 5.2 copy-start.10
  457.1 5.0 copy-start.24
  471.4 5.2 copy-start.10
  486.1 5.2 copy-start.10
  486.4 5.0 copy-start.24
  500.8 5.2 copy-start.10
  501.1 5.0 copy-start.24
  515.5 5.2 copy-start.10
  515.7 5.0 copy-start.24
  530.1 5.2 copy-start.10
  544.8 5.2 copy-start.10
  545.1 5.0 copy-start.24
  559.5 5.2 copy-start.10
  559.7 5.0 copy-start.24
  574.1 5.2 copy-start.10
  574.4 5.0 copy-start.24
  588.8 5.2 copy-start.10
  603.5 5.2 copy-start.10
  618.1 5.2 copy-start.10
  632.8 5.2 copy-start.10
  647.5 5.2 copy-start.10
  662.2 5.2 copy-start.10
  662.4 5.0 copy-start.24
  676.8 5.2 copy-start.10
  687.4 179.0 %all-reduce.9.cloned.1.call-start = ((), (), s32[]{:S(2)}) async-start(), calls=%async_computation.5 | async-start | bytes 6553600 | tf_op jit(solution)/shard_map/psum | solution.py:186
  (119 other events, 327.2 us)
Sparse Core Ops, SparseCore 0:
  12.2 59.0 all-gather.3
  271.1 73.0 all-reduce.4
  350.9 30.6 all-gather.5
  386.9 55.8 all-gather.7
  687.5 56.0 all-reduce.6
  756.9 109.4 all-reduce.8
where the time goes:
time: 881 us; the launch traced here: 879 us
  waiting for transfers between devices  369 us (42%)
  matrix products  286 us (32%)
  other arithmetic  135 us (15%)
  local copies, waits for them, and re-layouts  50.4 us (6%)
  loops' own time  23.5 us (3%)
  between operations  15.1 us (2%)
    dot_general x32, matrix products, absorb(): jnp.einsum('kgrj,jkd->kgrd', weights, value_float, precision=lax.Precisio...  142 us
    dot_general x32, matrix products, absorb(): jnp.einsum('rkgd,jkd->kgrj', heads_in, key_block, preferred_element_type=...  112 us
    psum x1, waiting for transfers between devices, on_device(): lax.psum(actor_grad.astype(jnp.bfloat16), ('rep', 'sec'))  109 us
    reduce_sum x32, other arithmetic, absorb(): row_sum = row_sum * rescale + jnp.sum(weights, axis=-1)  92.6 us
    psum x1, waiting for transfers between devices, on_device(): lax.psum(jnp.dot(attended, a_out, preferred_element_type=jnp.float32), 'm...  73.2 us
    all_gather x1, waiting for transfers between devices, on_device(): lax.all_gather(keyval, 'rep', axis=1, tiled=True)  53.9 us
    psum x1, waiting for transfers between devices, on_device(): lax.psum(jnp.dot(critic_attended, c_out, preferred_element_type=jnp.float...  52.2 us
    all_gather x1, waiting for transfers between devices, on_device(): lax.all_gather(critic_keyval, 'rep', axis=1, tiled=True)  49.4 us
  transfers between devices with their start and end apart: 6, of which 6 were waited for; matrix products, arithmetic and copies ran while one was open for 2% of the time, Pallas kernels for 0%

commit v1 on v0

--- a/solution.py
+++ b/solution.py
@@ -183,7 +183,9 @@
         "rh,rd->hd", critic_attended, dmixed_all, preferred_element_type=jnp.float32
     )
     actor_summed, critic_summed = (
-        lax.psum(actor_grad.astype(jnp.bfloat16), ("rep", "sec")).astype(jnp.float32),
+        jnp.sum(
+            jax.lax.all_gather(actor_grad.astype(jnp.bfloat16), axis_name=("rep", "sec")), 0
+        ).astype(jnp.float32),
         lax.psum(critic_grad.astype(jnp.bfloat16), ("rep", "sec")).astype(jnp.float32),
     )
     return (value_part[None, :], actor_summed, critic_summed)

time: 881 us -> 964 us (1.094)
  waiting for transfers between devices: 369 us -> 566 us
  matrix products: 286 us -> 229 us
  other arithmetic: 135 us -> 78.7 us
    all_gather x0 -> x1, waiting for transfers between devices: none -> 206 us  [on_device(): jax.lax.all_gather(actor_grad.astype(jnp.bfloat16), axis_name=('rep', 'se...]
    reduce_sum x32, other arithmetic: 92.6 us -> 22.1 us  [absorb(): row_sum = row_sum * rescale + jnp.sum(weights, axis=-1)]
    dot_general x32, matrix products: 112 us -> 53.4 us  [absorb(): jnp.einsum('rkgd,jkd->kgrj', heads_in, key_block, preferred_element_type=...]
    while x288 -> x32, local copies, waits for them, and re-layouts: 14.1 us -> 0.09 us
    reduce_sum x0 -> x1, other arithmetic: none -> 13 us  [on_device(): jnp.sum(jax.lax.all_gather(actor_grad.astype(jnp.bfloat16), axis_name=('r...]
    dynamic_slice x32, local copies, waits for them, and re-layouts: 18.8 us -> 30.8 us  [make_fold(): lax.scan(absorb, carried, (jnp.arange(block_count, dtype=jnp.int32), key_...]
  transfers between devices with their start and end apart: 6 -> 7, of which waited for: 6 -> 7; matrix products, arithmetic and copies ran while one was open for 2% -> 3% of each run, Pallas kernels for 0% -> 0%
where the time goes in v1:
time: 964 us; the launch traced here: 961 us
  waiting for transfers between devices  566 us (59%)
  matrix products  229 us (24%)
  other arithmetic  78.7 us (8%)
  local copies, waits for them, and re-layouts  49.5 us (5%)
  loops' own time  21.9 us (2%)
  between operations  15.1 us (2%)
    all_gather x1, waiting for transfers between devices, on_device(): jax.lax.all_gather(actor_grad.astype(jnp.bfloat16), axis_name=('rep', 'se...  206 us
    dot_general x32, matrix products, absorb(): jnp.einsum('kgrj,jkd->kgrd', weights, value_float, precision=lax.Precisio...  142 us
    psum x1, waiting for transfers between devices, on_device(): lax.psum(critic_grad.astype(jnp.bfloat16), ('rep', 'sec'))  100 us
    psum x1, waiting for transfers between devices, on_device(): lax.psum(jnp.dot(attended, a_out, preferred_element_type=jnp.float32), 'm...  73.2 us
    all_gather x1, waiting for transfers between devices, on_device(): lax.all_gather(keyval, 'rep', axis=1, tiled=True)  53.9 us
    dot_general x32, matrix products, absorb(): jnp.einsum('rkgd,jkd->kgrj', heads_in, key_block, preferred_element_type=...  53.4 us
    psum x1, waiting for transfers between devices, on_device(): lax.psum(jnp.dot(critic_attended, c_out, preferred_element_type=jnp.float...  52.2 us
    all_gather x1, waiting for transfers between devices, on_device(): lax.all_gather(critic_keyval, 'rep', axis=1, tiled=True)  49.3 us
  transfers between devices with their start and end apart: 7, of which 7 were waited for; matrix products, arithmetic and copies ran while one was open for 3% of the time, Pallas kernels for 0%

profile of v1, /device:TPU:1, one launch (start us, length us, event | category | flops | bytes accessed | tf_op | source)
XLA Modules:
  0.0 961.0 jit_solution(685229532629185302)
XLA Ops:
  17.4 53.9 %all-gather.6.cloned.1.call-done = bf16[2,8192,128]{2,1,0:T(8,128)(2,1)} async-done(((bf16[2,512,128]{2,1,0:T(8,128)(2,1)}), bf16[2,8192,128]{2,1,0:T(8,128)(2,1)}) %all-gather.6.cloned.1.call-update) | async-done | bytes 4194320 | tf_op jit(solution)/shard_map/all_gather | solution.py:152
  71.4 4.5 fusion.116
  75.9 129.9 %while.30 = (s32[]{:T(128)}, f32[1,3,512]{2,1,0:T(4,128)S(1)}, f32[1,3,512]{2,1,0:T(4,128)S(1)}, f32[1,3,512,128]{3,2,1,0:T(8,128)S(1)}, s32[16]{0:T(128)S(1)}, ...) while((s32[]{:T(128)}, f32[1,3,512]{2,1,0:T(4,128)S(1)}, ...), condition=%wide.region_4.5_spmd.clone, body=%wide.region_1.4_spmd.clone.sunk | while | flops 1415391232 | bytes 11765937 | solution.py:102
  104.3 3.9 fusion.148
  208.1 3.9 fusion.118
  212.1 73.2 %all-reduce.4.cloned.1.call-done = f32[512,1536]{1,0:T(8,128)} async-done(((f32[512,1536]{1,0:T(8,128)}), f32[512,1536]{1,0:T(8,128)}) %all-reduce.4.cloned.1.call-update) | async-done | bytes 3145744 | tf_op jit(solution)/shard_map/psum | solution.py:155
  291.9 30.8 %all-gather.8.cloned.1.call-done = bf16[512,2048]{1,0:T(8,128)(2,1)} async-done(((bf16[512,512]{1,0:T(8,128)(2,1)}), bf16[512,2048]{1,0:T(8,128)(2,1)}) %all-gather.8.cloned.1.call-update) | async-done | bytes 2097168 | tf_op jit(solution)/shard_map/all_gather | solution.py:162
  328.7 4.4 fusion.84
  335.1 49.3 %all-gather.10.cloned.1.call-done = bf16[2,8192,128]{2,1,0:T(8,128)(2,1)} async-done(((bf16[2,512,128]{2,1,0:T(8,128)(2,1)}), bf16[2,8192,128]{2,1,0:T(8,128)(2,1)}) %all-gather.10.cloned.1.call-update) | async-done | bytes 4194320 | tf_op jit(solution)/shard_map/all_gather | solution.py:170
  384.5 4.5 fusion.115
  389.5 161.6 %while.31 = (s32[]{:T(128)}, f32[1,4,512]{2,1,0:T(4,128)S(1)}, f32[1,4,512]{2,1,0:T(4,128)S(1)}, f32[1,4,512,128]{3,2,1,0:T(8,128)S(1)}, s32[16]{0:T(128)}, /*in...) while((s32[]{:T(128)}, f32[1,4,512]{2,1,0:T(4,128)S(1)}, ...), condition=%wide.region_10.11_spmd.clone, body=%wide.region_7.10_spmd.clone.sunk | while | flops 1887187968 | bytes 15599793 | solution.py:102
  394.6 4.9 fusion.153
  404.7 4.9 fusion.153
  414.9 4.9 fusion.153
  425.0 4.9 fusion.153
  435.1 4.9 fusion.153
  445.2 4.9 fusion.153
  455.3 4.9 fusion.153
  465.4 4.9 fusion.153
  475.5 4.9 fusion.153
  485.6 4.9 fusion.153
  495.7 4.9 fusion.153
  505.8 4.9 fusion.153
  515.9 4.9 fusion.153
  526.0 4.9 fusion.153
  536.1 4.9 fusion.153
  546.2 4.9 fusion.153
  560.5 52.2 %all-reduce.6.cloned.1.call-done = bf16[512,2048]{1,0:T(8,128)(2,1)} async-done(((bf16[512,2048]{1,0:T(8,128)(2,1)}), bf16[512,2048]{1,0:T(8,128)(2,1)}) %all-reduce.6.cloned.1.call-update) | async-done | bytes 2097168 | tf_op jit(solution)/shard_map/psum | solution.py:173
  628.9 100.4 %all-reduce.8.cloned.1.call-done = bf16[512,2048]{1,0:T(8,128)(2,1)} async-done(((bf16[512,2048]{1,0:T(8,128)(2,1)}), bf16[512,2048]{1,0:T(8,128)(2,1)}) %all-reduce.8.cloned.1.call-update) | async-done | bytes 2097168 | tf_op jit(solution)/shard_map/psum | solution.py:189
  729.2 4.1 convert_element_type.136
  733.4 206.2 %all-gather.12.cloned.1.call-done = bf16[12288,1536]{1,0:T(8,128)(2,1)} async-done(((bf16[384,1536]{1,0:T(8,128)(2,1)}), bf16[12288,1536]{1,0:T(8,128)(2,1)}) %all-gather.12.cloned.1.call-update) | async-done | bytes 37748752 | tf_op jit(solution)/shard_map/all_gather | solution.py:187
  939.5 13.0 %reduce_sum.132 = bf16[384,1536]{1,0:T(8,128)(2,1)S(1)} reduce(bf16[32,384,1536]{2,1,0:T(8,128)(2,1)} %bitcast.266, bf16[]{:T(256)} %constant.92.clone.1), dimensions={0}, to_apply=%region_19.20 | reduce | flops 18284544 | bytes 38928384 | tf_op jit(solution)/shard_map/reduce_sum | solution.py:186
  (331 shorter events, 240.8 us)
Async XLA Ops:
  7.2 546.7 %copy-start = (bf16[512,2048]{1,0:T(8,128)(2,1)S(1)}, bf16[512,2048]{1,0:T(8,128)(2,1)}, u32[]{:S(2)}) copy-start(bf16[512,2048]{1,0:T(8,128)(2,1)} %param.27) | copy-start | bytes 6291460
  7.2 64.2 %all-gather.6.cloned.1.call-start = ((), (), s32[]{:S(2)}) async-start(), calls=%async_computation | async-start | bytes 4456448 | tf_op jit(solution)/shard_map/all_gather | solution.py:152
  12.1 4.7 copy-start.14
  12.1 273.2 %all-reduce.4.cloned.1.call-start = ((), (), s32[]{:S(2)}) async-start(), calls=%async_computation.1 | async-start | bytes 6291456 | tf_op jit(solution)/shard_map/psum | solution.py:155
  212.1 110.6 %all-gather.8.cloned.1.call-start = ((), (), s32[]{:S(2)}) async-start(), calls=%async_computation.2 | async-start | bytes 2621440 | tf_op jit(solution)/shard_map/all_gather | solution.py:162
  285.3 4.7 copy-start.12
  288.9 1.1 copy-start.2
  290.1 35.3 %copy-start.13 = (bf16[2,2048,128]{2,1,0:T(8,128)(2,1)S(1)}, bf16[2,2048,128]{2,1,0:T(8,128)(2,1)}, u32[]{:S(2)}) copy-start(bf16[2,2048,128]{2,1,0:T(8,128)(2,1)} %param.26) | copy-start | bytes 3145732
  291.9 92.6 %all-gather.10.cloned.1.call-start = ((), (), s32[]{:S(2)}) async-start(), calls=%async_computation.3 | async-start | bytes 4456448 | tf_op jit(solution)/shard_map/all_gather | solution.py:170
  324.8 0.6 copy-start.10
  328.4 284.3 %all-reduce.6.cloned.1.call-start = ((), (), s32[]{:S(2)}) async-start(), calls=%async_computation.4 | async-start | bytes 4194304 | tf_op jit(solution)/shard_map/psum | solution.py:173
  553.8 2.9 copy-start.15
  553.9 3.6 copy-start.5
  553.9 4.2 copy-start.7
  556.5 3.9 copy-start.6
  556.5 172.7 %all-reduce.8.cloned.1.call-start = ((), (), s32[]{:S(2)}) async-start(), calls=%async_computation.5 | async-start | bytes 4194304 | tf_op jit(solution)/shard_map/psum | solution.py:189
  612.7 3.2 copy-start.1
  612.7 3.5 copy-start.4
  615.8 1.2 copy-start.11
  618.7 3.2 copy-start.8
  618.8 3.2 copy-start.9
  621.8 317.7 %all-gather.12.cloned.1.call-start = ((), (), s32[]{:S(2)}) async-start(), calls=%async_computation.6 | async-start | bytes 38928384 | tf_op jit(solution)/shard_map/all_gather | solution.py:187
  621.9 4.4 copy-start.3
Sparse Core Ops, SparseCore 0:
  12.2 59.0 all-gather.5
  212.2 73.0 all-reduce.3
  292.0 30.6 all-gather.7
  328.5 55.8 all-gather.9
  556.6 56.0 all-reduce.5
  622.0 107.2 all-reduce.7
  731.0 208.4 all-gather.11
